TPU v7x, 32 devices: a whole 2x2x4 slice. The times are simulated.
32 devices in a mesh: dp: 4 (over y, x), ctx: 8 (over z, core).
Axes of the slice: x: 2, y: 2, z: 4, core: 2. Of those that a mesh axis runs over, the one named last changes fastest.
Arguments:
- hidden_in: bfloat16 [8, 512, 2048], P('dp', 'ctx'), may hold values from -6 to 6
- segment_ids: int32 [8, 512], P('dp', 'ctx'), may hold values from 0 to 10, as said below
- norm1_gain: bfloat16 [2048], P(('dp', 'ctx')), may hold values from 0.25 to 1.75
- norm1_bias: bfloat16 [2048], P(('dp', 'ctx')), may hold values from -2 to 2
- qkv_weight: bfloat16 [2048, 6144], P(('dp', 'ctx')), may hold values from -0.125 to 0.125
- qkv_bias: bfloat16 [6144], P(('dp', 'ctx')), may hold values from -2 to 2
- out_weight: bfloat16 [2048, 2048], P(('dp', 'ctx')), may hold values from -0.5 to 0.5
- norm2_gain: bfloat16 [2048], P(('dp', 'ctx')), may hold values from 0.25 to 1.75
- norm2_bias: bfloat16 [2048], P(('dp', 'ctx')), may hold values from -2 to 2
- gate_up_weight: bfloat16 [2048, 11264], P(('dp', 'ctx')), may hold values from -0.125 to 0.125
- down_weight: bfloat16 [2048, 5632], P(('dp', 'ctx')), may hold values from -0.109375 to 0.109375
- out_grad: bfloat16 [8, 512, 2048], P('dp', 'ctx'), may hold values from -6 to 6
Outputs:
- hidden_out: bfloat16 [8, 512, 2048], P('dp', 'ctx')
- hidden_in_grad: bfloat16 [8, 512, 2048], P('dp', 'ctx')
- norm1_gain_grad: float32 [2048], P(('dp', 'ctx'))
- norm1_bias_grad: float32 [2048], P(('dp', 'ctx'))
- qkv_weight_grad: float32 [2048, 6144], P(('dp', 'ctx'))
- qkv_bias_grad: float32 [6144], P(('dp', 'ctx'))
- out_weight_grad: float32 [2048, 2048], P(('dp', 'ctx'))
- norm2_gain_grad: float32 [2048], P(('dp', 'ctx'))
- norm2_bias_grad: float32 [2048], P(('dp', 'ctx'))
- gate_up_weight_grad: float32 [2048, 11264], P(('dp', 'ctx'))
- down_weight_grad: float32 [2048, 5632], P(('dp', 'ctx'))
Inputs may be any that keep to these rules, and one draw needn't show every extreme that they name: `segment_ids`: within each sequence the ids start at 0 and rise by one at each document boundary; every document but the last of a sequence has 51 tokens or more; of the 2 sequences of each dp index, one has exactly two documents, the last of 51 tokens; one sequence in all has every document but its last of exactly 51 tokens.
All inputs are finite; a program needn't handle non-finite values.
Results may differ from a plain program's by a relative error of at most 0.015.
Values may be sent and summed in bfloat16 or wider, within the bound.
No kernel may reach another device: no remote copies, remote signals or barrier semaphores. Data moves between devices by JAX's collectives and lax.ppermute only.
A program may use at most 704 MiB of HBM per device.

v0:
```python
import jax
import jax.numpy as jnp
from jax import lax
from jax.sharding import PartitionSpec as P

D = 2048
HEADS = 32
HEAD = 64
ROT = 16
FF = 5632


epsilon = 1e-05
very_low = -1e30


def statistics(values):
    average = jnp.mean(values, axis=-1, keepdims=True)
    centred = values - average
    spread = jnp.mean(centred * centred, axis=-1, keepdims=True)
    scaling = lax.rsqrt(spread + epsilon)
    return (centred * scaling, scaling)


def norm_back(grad_hat, normal, scaling):
    first = jnp.mean(grad_hat, axis=-1, keepdims=True)
    second = jnp.mean(grad_hat * normal, axis=-1, keepdims=True)
    return scaling * (grad_hat - first - normal * second)


def rotate(values, cosine_table, sine_table):
    half_rot = ROT // 2
    first = values[..., :half_rot]
    second = values[..., half_rot:ROT]
    return jnp.concatenate(
        [
            first * cosine_table - second * sine_table,
            second * cosine_table + first * sine_table,
            values[..., ROT:],
        ],
        axis=-1,
    )


def rotate_back(values, cosine_table, sine_table):
    half_rot = ROT // 2
    first = values[..., :half_rot]
    second = values[..., half_rot:ROT]
    return jnp.concatenate(
        [
            first * cosine_table + second * sine_table,
            second * cosine_table - first * sine_table,
            values[..., ROT:],
        ],
        axis=-1,
    )


def visible(query_pos, query_seg, key_pos, key_seg):
    causal = key_pos[None, None, :] <= query_pos[None, :, None]
    same_doc = key_seg[:, None, :] == query_seg[:, :, None]
    return (causal & same_doc)[:, None]


def contract_last(left_rows, right_rows):
    return lax.dot_general(
        left_rows, right_rows, (((1,), (1,)), ((), ())), preferred_element_type=jnp.float32
    )


def block_length(piece_len):
    sub_len = piece_len
    while sub_len > 512 and sub_len % 2 == 0:
        sub_len = sub_len // 2
    return sub_len


def on_device(
    hidden_in,
    segment_ids,
    norm1_gain,
    norm1_bias,
    qkv_weight,
    qkv_bias,
    out_weight,
    norm2_gain,
    norm2_bias,
    gate_up_weight,
    down_weight,
    out_grad,
):
    seq_count, span_len, model_width = hidden_in.shape
    row_count = seq_count * span_len
    own_rows = qkv_weight.shape[0]
    score_scale = HEAD ** (-0.5)
    inputs = hidden_in.reshape(row_count, model_width).astype(jnp.float32)
    places = lax.axis_index("ctx") * span_len + jnp.arange(span_len, dtype=jnp.int32)
    frequency = 10000.0 ** (-jnp.arange(ROT // 2).astype(jnp.float32) * 2.0 / ROT)
    angles = places.astype(jnp.float32)[:, None] * frequency[None, :]
    cosine_table = jnp.cos(angles)[None, :, None, :]
    sine_table = jnp.sin(angles)[None, :, None, :]
    normal_one, scale_one = statistics(inputs)
    gain_piece = lax.all_gather(norm1_gain, ("dp", "ctx"), axis=0, tiled=True)
    bias_piece = lax.all_gather(norm1_bias, ("dp", "ctx"), axis=0, tiled=True)
    weight_piece = lax.all_gather(qkv_weight, ("dp", "ctx"), axis=0, tiled=True)
    extra_piece = lax.all_gather(qkv_bias.reshape(own_rows, 3), ("dp", "ctx"), axis=0, tiled=True)
    columns = normal_one
    scaled = (columns * gain_piece.astype(jnp.float32) + bias_piece.astype(jnp.float32)).astype(
        jnp.bfloat16
    )
    running = jnp.dot(scaled, weight_piece, preferred_element_type=jnp.float32)
    normed = scaled
    gains = gain_piece.astype(jnp.float32)
    biases = extra_piece.astype(jnp.float32)
    mixed_one = running
    normed_one = normed
    gain_one = gains
    mixed_one = mixed_one + biases.reshape(3 * D)
    shaped = mixed_one.reshape(seq_count, span_len, 3, HEADS, HEAD)
    queries = rotate(shaped[:, :, 0], cosine_table, sine_table).astype(jnp.bfloat16)
    key_rot = rotate(shaped[:, :, 1], cosine_table, sine_table).astype(jnp.bfloat16)
    value_rot = shaped[:, :, 2].astype(jnp.bfloat16)
    key_flat = key_rot.reshape(seq_count, span_len, D)
    value_flat = value_rot.reshape(seq_count, span_len, D)
    start_att = (
        jnp.full((seq_count, HEADS, span_len), very_low, jnp.float32),
        jnp.zeros((seq_count, HEADS, span_len), jnp.float32),
        jnp.zeros((seq_count, HEADS, span_len, HEAD), jnp.float32),
    )
    key_piece = lax.all_gather(key_flat, "ctx", axis=1, tiled=True)
    value_piece = lax.all_gather(value_flat, "ctx", axis=1, tiled=True)
    seg_piece = lax.all_gather(segment_ids, "ctx", axis=1, tiled=True)
    piece_len = key_piece.shape[1]
    sub_len = block_length(piece_len)

    def attend_one_step(block_index, state_now):
        first_key = block_index * sub_len
        key_heads = lax.dynamic_slice_in_dim(key_piece, first_key, sub_len, 1).reshape(
            seq_count, sub_len, HEADS, HEAD
        )
        value_heads = lax.dynamic_slice_in_dim(value_piece, first_key, sub_len, 1).reshape(
            seq_count, sub_len, HEADS, HEAD
        )
        seg_part = lax.dynamic_slice_in_dim(seg_piece, first_key, sub_len, 1)
        allowed = visible(
            places, segment_ids, first_key + jnp.arange(sub_len, dtype=jnp.int32), seg_part
        )
        running_max, running_sum, summed = state_now
        scores = (
            jnp.einsum("sqhd,skhd->shqk", queries, key_heads, preferred_element_type=jnp.float32)
            * score_scale
        )
        masked = jnp.where(allowed, scores, very_low)
        new_max = jnp.maximum(running_max, jnp.max(masked, axis=-1))
        weights = jnp.where(allowed, jnp.exp(masked - new_max[..., None]), 0.0)
        factor = jnp.exp(running_max - new_max)
        running_sum = running_sum * factor + jnp.sum(weights, axis=-1)
        summed = summed * factor[..., None] + jnp.einsum(
            "shqk,skhd->shqd", weights, value_heads.astype(jnp.float32)
        )
        return (new_max, running_sum, summed)

    running_max, running_sum, summed = lax.fori_loop(
        0, piece_len // sub_len, attend_one_step, start_att
    )
    out_heads = jnp.transpose(summed / running_sum[..., None], (0, 2, 1, 3))
    log_total = running_max + jnp.log(running_sum)
    attended_low = out_heads.reshape(row_count, D).astype(jnp.bfloat16)
    columns = attended_low
    projected = jnp.dot(
        columns,
        lax.all_gather(out_weight, ("dp", "ctx"), axis=0, tiled=True),
        preferred_element_type=jnp.float32,
    )
    middle = inputs + projected
    normal_two, scale_two = statistics(middle)
    gain_piece = lax.all_gather(norm2_gain, ("dp", "ctx"), axis=0, tiled=True)
    bias_piece = lax.all_gather(norm2_bias, ("dp", "ctx"), axis=0, tiled=True)
    weight_piece = lax.all_gather(gate_up_weight, ("dp", "ctx"), axis=0, tiled=True)
    columns = normal_two
    scaled = (columns * gain_piece.astype(jnp.float32) + bias_piece.astype(jnp.float32)).astype(
        jnp.bfloat16
    )
    running = jnp.dot(scaled, weight_piece, preferred_element_type=jnp.float32)
    normed = scaled
    gains = gain_piece.astype(jnp.float32)
    gate_pre = running[:, :FF]
    up_pre = running[:, FF:]
    hidden = (jax.nn.silu(gate_pre) * up_pre).astype(jnp.bfloat16)
    branch = contract_last(hidden, lax.all_gather(down_weight, ("dp", "ctx"), axis=0, tiled=True))
    result = (middle + branch).astype(jnp.bfloat16).reshape(seq_count, span_len, model_width)
    grad_out = out_grad.reshape(row_count, model_width)
    grad_f = grad_out.astype(jnp.float32)
    columns = grad_out
    grad_hidden = jnp.dot(
        columns,
        lax.all_gather(down_weight, ("dp", "ctx"), axis=0, tiled=True),
        preferred_element_type=jnp.float32,
    )
    sigmoid_gate = jax.nn.sigmoid(gate_pre)
    grad_gate = grad_hidden * up_pre * sigmoid_gate * (1.0 + gate_pre * (1.0 - sigmoid_gate))
    grad_up = grad_hidden * gate_pre * sigmoid_gate
    grad_mixed_two = jnp.concatenate([grad_gate, grad_up], axis=1).astype(jnp.bfloat16)
    mlp_parts = ((normed, grad_mixed_two), (grad_out, hidden))
    mlp_sums = None
    grad_normed_two = contract_last(
        grad_mixed_two, lax.all_gather(gate_up_weight, ("dp", "ctx"), axis=0, tiled=True)
    )
    gain_two_grad = jnp.sum(grad_normed_two * normal_two, axis=0)
    bias_two_grad = jnp.sum(grad_normed_two, axis=0)
    grad_middle = grad_f + norm_back(grad_normed_two * gains, normal_two, scale_two)
    grad_projected = grad_middle.astype(jnp.bfloat16)
    grad_attended = contract_last(
        grad_projected, lax.all_gather(out_weight, ("dp", "ctx"), axis=0, tiled=True)
    ).astype(jnp.bfloat16)
    grad_heads = grad_attended.reshape(seq_count, span_len, HEADS, HEAD)
    delta_rows = jnp.sum(grad_heads.astype(jnp.float32) * out_heads, axis=-1)
    delta_heads = jnp.transpose(delta_rows, (0, 2, 1))
    query_key_piece = lax.all_gather(key_flat, "ctx", axis=1, tiled=True)
    query_value_piece = lax.all_gather(value_flat, "ctx", axis=1, tiled=True)
    query_seg_piece = lax.all_gather(segment_ids, "ctx", axis=1, tiled=True)
    piece_len = query_key_piece.shape[1]
    query_sub_len = block_length(piece_len)

    def query_one_step(block_index, state_now):
        first_key = block_index * query_sub_len
        key_heads = lax.dynamic_slice_in_dim(query_key_piece, first_key, query_sub_len, 1).reshape(
            seq_count, query_sub_len, HEADS, HEAD
        )
        value_heads = lax.dynamic_slice_in_dim(
            query_value_piece, first_key, query_sub_len, 1
        ).reshape(seq_count, query_sub_len, HEADS, HEAD)
        seg_part = lax.dynamic_slice_in_dim(query_seg_piece, first_key, query_sub_len, 1)
        allowed = visible(
            places, segment_ids, first_key + jnp.arange(query_sub_len, dtype=jnp.int32), seg_part
        )
        scores = (
            jnp.einsum("sqhd,skhd->shqk", queries, key_heads, preferred_element_type=jnp.float32)
            * score_scale
        )
        probability = jnp.where(allowed, jnp.exp(scores - log_total[..., None]), 0.0)
        pushes = jnp.einsum(
            "sqhd,skhd->shqk", grad_heads, value_heads, preferred_element_type=jnp.float32
        )
        slopes = probability * (pushes - delta_heads[..., None])
        return (
            state_now
            + jnp.einsum("shqk,skhd->sqhd", slopes, key_heads.astype(jnp.float32)) * score_scale
        )

    grad_queries = lax.fori_loop(
        0,
        piece_len // query_sub_len,
        query_one_step,
        jnp.zeros((seq_count, span_len, HEADS, HEAD), jnp.float32),
    )
    total_rows = jnp.transpose(log_total, (0, 2, 1))
    all_totals, all_deltas = (
        lax.all_gather(total_rows, "ctx", axis=1, tiled=True),
        lax.all_gather(delta_rows, "ctx", axis=1, tiled=True),
    )
    send_queries = queries.reshape(seq_count, span_len, D)
    send_pushes = grad_attended.reshape(seq_count, span_len, D)
    start_keys = (
        jnp.zeros((seq_count, span_len, HEADS, HEAD), jnp.float32),
        jnp.zeros((seq_count, span_len, HEADS, HEAD), jnp.float32),
    )
    query_piece = lax.all_gather(send_queries, "ctx", axis=1, tiled=True)
    push_piece = lax.all_gather(send_pushes, "ctx", axis=1, tiled=True)
    key_seg_piece = lax.all_gather(segment_ids, "ctx", axis=1, tiled=True)
    piece_len = query_piece.shape[1]
    key_sub_len = block_length(piece_len)

    def key_one_step(block_index, state_now):
        first_row = block_index * key_sub_len
        query_heads = lax.dynamic_slice_in_dim(query_piece, first_row, key_sub_len, 1).reshape(
            seq_count, key_sub_len, HEADS, HEAD
        )
        push_heads = lax.dynamic_slice_in_dim(push_piece, first_row, key_sub_len, 1).reshape(
            seq_count, key_sub_len, HEADS, HEAD
        )
        seg_part = lax.dynamic_slice_in_dim(key_seg_piece, first_row, key_sub_len, 1)
        total_part = lax.dynamic_slice_in_dim(all_totals, first_row, key_sub_len, 1)
        delta_part = lax.dynamic_slice_in_dim(all_deltas, first_row, key_sub_len, 1)
        allowed = visible(
            first_row + jnp.arange(key_sub_len, dtype=jnp.int32), seg_part, places, segment_ids
        )
        grad_keys, grad_values = state_now
        scores = (
            jnp.einsum("sqhd,skhd->shqk", query_heads, key_rot, preferred_element_type=jnp.float32)
            * score_scale
        )
        probability = jnp.where(
            allowed, jnp.exp(scores - jnp.transpose(total_part, (0, 2, 1))[..., None]), 0.0
        )
        pushes = jnp.einsum(
            "sqhd,skhd->shqk", push_heads, value_rot, preferred_element_type=jnp.float32
        )
        slopes = probability * (pushes - jnp.transpose(delta_part, (0, 2, 1))[..., None])
        grad_values = grad_values + jnp.einsum(
            "shqk,sqhd->skhd", probability, push_heads.astype(jnp.float32)
        )
        grad_keys = (
            grad_keys
            + jnp.einsum("shqk,sqhd->skhd", slopes, query_heads.astype(jnp.float32)) * score_scale
        )
        return (grad_keys, grad_values)

    grad_keys, grad_values = lax.fori_loop(0, piece_len // key_sub_len, key_one_step, start_keys)
    grad_q = rotate_back(grad_queries, cosine_table, sine_table)
    grad_k = rotate_back(grad_keys, cosine_table, sine_table)
    grad_mixed_one = (
        jnp.stack([grad_q, grad_k, grad_values], axis=2)
        .reshape(row_count, 3 * D)
        .astype(jnp.bfloat16)
    )
    qkv_bias_full = jnp.sum(grad_mixed_one.astype(jnp.float32), axis=0)
    grad_normed_one = contract_last(
        grad_mixed_one, lax.all_gather(qkv_weight, ("dp", "ctx"), axis=0, tiled=True)
    )
    gain_one_grad = jnp.sum(grad_normed_one * normal_one, axis=0)
    bias_one_grad = jnp.sum(grad_normed_one, axis=0)
    grad_inputs = grad_middle + norm_back(grad_normed_one * gain_one, normal_one, scale_one)
    grad_result = grad_inputs.astype(jnp.bfloat16).reshape(seq_count, span_len, model_width)
    attn_parts = ((normed_one, grad_mixed_one), (attended_low, grad_projected))
    grad_parts = attn_parts + mlp_parts
    joined = lax.psum_scatter(
        jnp.concatenate(
            [
                lax.dot_general(
                    left_rows,
                    right_rows,
                    (((0,), (0,)), ((), ())),
                    preferred_element_type=jnp.float32,
                )
                for left_rows, right_rows in grad_parts
            ],
            axis=1,
        ),
        ("dp", "ctx"),
        scatter_dimension=0,
        tiled=True,
    )
    attn_sums = joined[:, : 4 * D]
    mlp_sums = joined[:, 4 * D :]
    small_sums = (
        lax.psum_scatter(gain_one_grad, ("dp", "ctx"), scatter_dimension=0, tiled=True),
        lax.psum_scatter(bias_one_grad, ("dp", "ctx"), scatter_dimension=0, tiled=True),
        lax.psum_scatter(qkv_bias_full, ("dp", "ctx"), scatter_dimension=0, tiled=True),
        lax.psum_scatter(gain_two_grad, ("dp", "ctx"), scatter_dimension=0, tiled=True),
        lax.psum_scatter(bias_two_grad, ("dp", "ctx"), scatter_dimension=0, tiled=True),
    )
    return (
        result,
        grad_result,
        small_sums[0],
        small_sums[1],
        attn_sums[:, : 3 * D],
        small_sums[2],
        attn_sums[:, 3 * D :],
        small_sums[3],
        small_sums[4],
        mlp_sums[:, : 2 * FF],
        mlp_sums[:, 2 * FF :],
    )


def solution(mesh):
    placed = (
        P("dp", "ctx", None),
        P("dp", "ctx"),
        P(("dp", "ctx")),
        P(("dp", "ctx")),
        P(("dp", "ctx"), None),
        P(("dp", "ctx")),
        P(("dp", "ctx"), None),
        P(("dp", "ctx")),
        P(("dp", "ctx")),
        P(("dp", "ctx"), None),
        P(("dp", "ctx"), None),
        P("dp", "ctx", None),
    )
    return jax.shard_map(
        on_device,
        mesh=mesh,
        in_specs=placed,
        out_specs=(
            P("dp", "ctx", None),
            P("dp", "ctx", None),
            P(("dp", "ctx")),
            P(("dp", "ctx")),
            P(("dp", "ctx"), None),
            P(("dp", "ctx")),
            P(("dp", "ctx"), None),
            P(("dp", "ctx")),
            P(("dp", "ctx")),
            P(("dp", "ctx"), None),
            P(("dp", "ctx"), None),
        ),
        check_vma=False,
    )
```

profile of v0, /device:TPU:0, one launch (start us, length us, event | category | flops | bytes accessed | tf_op | source)
XLA Modules:
  0.0 3330.7 jit_solution(17834366810322769696)
XLA Ops:
  14.1 43.2 %all-reduce.10 = (bf16[2048]{0:T(1024)(128)(2,1)S(1)}, bf16[2048]{0:T(1024)(128)(2,1)S(1)}, bf16[2048]{0:T(1024)(128)(2,1)S(1)}, bf16[2048]{0:T(1024)(128)(2,1)S(1)}) all-reduce(bf16[2048]{0:T(1024)(128)(2,1)S(1)} %dynamic-update-slice.1, bf16[2048]{0:T(1024)(128)(2,1)S(1)} %dynamic-update-slice, ...), channel_id=1, replica_groups=mesh['dp'=4,'ctx'=8] {'dp','ctx'}, use_global_device_ids=true, to_apply=%add.1 | all-reduce | flops 8192 | bytes 32768
  58.5 40.7 %all-gather.1 = bf16[32,64,3]{1,2,0:T(4,128)(2,1)S(1)} all-gather(bf16[1,64,3]{1,2,0:T(4,128)(2,1)S(1)} %copy.130), channel_id=1, replica_groups=mesh['dp'=4,'ctx'=8] {'dp','ctx'}, dimensions={0}, use_global_device_ids=true | all-gather | bytes 12672 | tf_op jit(solution)/shard_map/all_gather | solution.py:106
  100.7 69.5 %all-gather.11.cloned.1.call-done = bf16[2048,6144]{1,0:T(8,128)(2,1)} async-done(((bf16[64,6144]{1,0:T(8,128)(2,1)}), bf16[2048,6144]{1,0:T(8,128)(2,1)}) %all-gather.11.cloned.1.call-update) | async-done | bytes 25165840 | tf_op jit(solution)/shard_map/all_gather | solution.py:105
  170.2 13.3 convolution_add_fusion
  231.2 15.8 all-gather.13.cloned.1.call-done
  260.4 17.1 all_gather.69
  278.3 20.9 all-gather.15.cloned.1.call-done
  299.2 11.3 copy.142
  322.6 24.5 all-gather.23.cloned.1.call-done
  353.4 72.8 %all-gather.17.cloned.1.call-done = bf16[2048,2048]{1,0:T(8,128)(2,1)} async-done(((bf16[64,2048]{1,0:T(8,128)(2,1)}), bf16[2048,2048]{1,0:T(8,128)(2,1)}) %all-gather.17.cloned.1.call-update) | async-done | bytes 8388624 | tf_op jit(solution)/shard_map/all_gather | solution.py:172
  437.0 245.8 %all-gather.19.cloned.1.call-done = bf16[2048,11264]{1,0:T(8,128)(2,1)} async-done(((bf16[64,11264]{1,0:T(8,128)(2,1)}), bf16[2048,11264]{1,0:T(8,128)(2,1)}) %all-gather.19.cloned.1.call-update) | async-done | bytes 46137360 | tf_op jit(solution)/shard_map/all_gather | solution.py:179
  682.8 20.7 fusion.65
  703.5 125.0 %all-gather.21.cloned.1.call-done = bf16[2048,5632]{1,0:T(8,128)(2,1)} async-done(((bf16[64,5632]{1,0:T(8,128)(2,1)}), bf16[2048,5632]{1,0:T(8,128)(2,1)}) %all-gather.21.cloned.1.call-update) | async-done | bytes 23068688 | tf_op jit(solution)/shard_map/all_gather | solution.py:190
  828.5 13.0 multiply_convert_fusion.1
  841.5 23.4 multiply_reduce_fusion.1
  893.9 18.7 all_gather.71
  926.6 17.8 convolution_bitcast_fusion
  944.4 33.5 %fusion.38 = f32[2048,11264]{1,0:T(8,128)} fusion(bf16[128,5632]{1,0:T(8,128)(2,1)} %get-tuple-element.126, bf16[128,5632]{1,0:T(8,128)(2,1)} %get-tuple-element.125, f32[128,2048]{1,0:T(8,128)S(1)} %get-tuple-element.165, f32[2048]{0:T(1024)S(1)} %convert_element_type.145, f32[2048]{0:T(1024)S(1)} %convert_element_type.144, f32[128]{0:T(128)S(1)} %copy-done.36, ...), kind=kOutput, calls=%fused_computation.71 | convolution fusion | flops 5912657920 | bytes 96224256 | tf_op jit(solution)/shard_map/dot_general | solution.py:330
  1014.7 19.4 fusion.71
  1034.1 132.9 %pad_maximum_fusion = f32[2048,25088]{1,0:T(8,128)} fusion(f32[2048,5632]{1,0:T(8,128)} %convolution_bitcast_fusion, f32[2048,11264]{1,0:T(8,128)} %fusion.38, f32[2048,2048]{1,0:T(8,128)} %fusion.48, f32[2048,6144]{1,0:T(8,128)} %fusion.71), kind=kLoop, calls=%fused_computation | loop fusion | flops 154140672 | bytes 411041792 | tf_op jit(solution)/shard_map/concatenate | solution.py:328
  1168.2 14.4 fusion.36
  1182.7 14.7 multiply_reduce_fusion.2
  1197.4 40.6 %all-reduce.9 = (f32[2048]{0:T(1024)S(1)}, f32[2048]{0:T(1024)S(1)}, f32[6144]{0:T(1024)S(1)}, f32[2048]{0:T(1024)S(1)}, f32[2048]{0:T(1024)S(1)}) all-reduce(f32[2048]{0:T(1024)S(1)} %get-tuple-element.95, f32[2048]{0:T(1024)S(1)} %get-tuple-element.100, ...), channel_id=2, replica_groups=mesh['dp'=4,'ctx'=8] {'dp','ctx'}, use_global_device_ids=true, to_apply=%region_12.13.clone | all-reduce | flops 14336 | bytes 114688
  1243.5 2069.7 %reduce-scatter.2.cloned.1.call-done = f32[64,25088]{1,0:T(8,128)} async-done(((f32[2048,25088]{1,0:T(8,128)}), f32[64,25088]{1,0:T(8,128)}) %reduce-scatter.2.cloned.1.call-update) | async-done | bytes 6422544 | tf_op jit(solution)/shard_map/reduce_scatter | solution.py:327
  (215 shorter events, 197.4 us)
Async XLA Ops:
  7.2 93.1 %copy-start.3 = (bf16[2,64,2048]{2,1,0:T(8,128)(2,1)S(1)}, bf16[2,64,2048]{2,1,0:T(8,128)(2,1)}, u32[]{:S(2)}) copy-start(bf16[2,64,2048]{2,1,0:T(8,128)(2,1)} %param.12) | copy-start | bytes 1572868
  7.2 163.0 %all-gather.11.cloned.1.call-start = ((), (), s32[]{:S(2)}) async-start(), calls=%async_computation.1 | async-start | bytes 25952256 | tf_op jit(solution)/shard_map/all_gather | solution.py:105
  7.9 239.0 %all-gather.13.cloned.1.call-start = ((), (), s32[]{:S(2)}) async-start(), calls=%async_computation.2 | async-start | bytes 4718592 | tf_op jit(solution)/shard_map/all_gather | solution.py:130
  9.3 174.2 %copy-start.41 = (f32[128]{0:T(128)}, f32[128]{0:T(128)S(1)}, u32[]{:S(2)}) copy-start(f32[128]{0:T(128)S(1)} %div.46) | copy-start | bytes 1540
  10.7 172.8 %copy-start.43 = (f32[128]{0:T(128)}, f32[128]{0:T(128)S(1)}, u32[]{:S(2)}) copy-start(f32[128]{0:T(128)S(1)} %rsqrt.21) | copy-start | bytes 1540
  57.3 172.7 %copy-start.26 = (f32[2048]{0:T(1024)}, f32[2048]{0:T(1024)S(1)}, u32[]{:S(2)}) copy-start(f32[2048]{0:T(1024)S(1)} %convert_element_type.132) | copy-start | bytes 24580
  58.4 137.0 %copy-start.22 = (f32[64,8]{1,0:T(8,128)}, f32[64,8]{1,0:T(8,128)S(1)}, u32[]{:S(2)}) copy-start(f32[64,8]{1,0:T(8,128)S(1)} %copy.134) | copy-start | bytes 6148
  58.5 136.9 %copy-start.24 = (f32[64,8]{1,0:T(8,128)}, f32[64,8]{1,0:T(8,128)S(1)}, u32[]{:S(2)}) copy-start(f32[64,8]{1,0:T(8,128)S(1)} %copy.135) | copy-start | bytes 6148
  201.5 97.7 %all-gather.15.cloned.1.call-start = ((), (), s32[]{:S(2)}) async-start(), calls=%async_computation.3 | async-start | bytes 4718592 | tf_op jit(solution)/shard_map/all_gather | solution.py:131
  207.0 140.2 %all-gather.23.cloned.1.call-start = ((), (), s32[]{:S(2)}) async-start(), calls=%async_computation.7 | async-start | bytes 4718592 | tf_op jit(solution)/shard_map/all_gather | solution.py:268
  216.8 209.4 %all-gather.17.cloned.1.call-start = ((), (), s32[]{:S(2)}) async-start(), calls=%async_computation.4 | async-start | bytes 8650752 | tf_op jit(solution)/shard_map/all_gather | solution.py:172
  217.4 465.4 %all-gather.19.cloned.1.call-start = ((), (), s32[]{:S(2)}) async-start(), calls=%async_computation.5 | async-start | bytes 47579136 | tf_op jit(solution)/shard_map/all_gather | solution.py:179
  217.9 610.5 %all-gather.21.cloned.1.call-start = ((), (), s32[]{:S(2)}) async-start(), calls=%async_computation.6 | async-start | bytes 23789568 | tf_op jit(solution)/shard_map/all_gather | solution.py:190
  218.7 759.3 %all-gather.25.cloned.1.call-start = ((), (), s32[]{:S(2)}) async-start(), calls=%async_computation.8 | async-start | bytes 4718592 | tf_op jit(solution)/shard_map/all_gather | solution.py:269
  229.2 81.3 %copy-start.21 = (pred[2,64,512]{2,1,0:T(8,128)(4,1)}, pred[2,64,512]{2,1,0:T(8,128)(4,1)S(1)}, u32[]{:S(2)}) copy-start(pred[2,64,512]{2,1,0:T(8,128)(4,1)S(1)} %compare_and_fusion.1) | copy-start | bytes 196612
  322.6 103.5 %copy-start.13 = (bf16[128,2048]{1,0:T(8,128)(2,1)}, bf16[128,2048]{1,0:T(8,128)(2,1)S(1)}, u32[]{:S(2)}) copy-start(bf16[128,2048]{1,0:T(8,128)(2,1)S(1)} %convert_element_type.143) | copy-start | bytes 1572868
  431.0 513.4 %copy-start = (f32[128,2048]{1,0:T(8,128)}, f32[128,2048]{1,0:T(8,128)S(1)}, u32[]{:S(2)}) copy-start(f32[128,2048]{1,0:T(8,128)S(1)} %get-tuple-element.165) | copy-start | bytes 3145732
  431.1 251.7 %copy-start.31 = (f32[128]{0:T(128)}, f32[128]{0:T(128)S(1)}, u32[]{:S(2)}) copy-start(f32[128]{0:T(128)S(1)} %broadcast_multiply_fusion.5) | copy-start | bytes 1540
  431.3 251.4 %copy-start.34 = (f32[128]{0:T(128)}, f32[128]{0:T(128)S(1)}, u32[]{:S(2)}) copy-start(f32[128]{0:T(128)S(1)} %add_rsqrt_fusion.1) | copy-start | bytes 1540
  437.0 391.5 %copy-start.18 = (bf16[2,64,2048]{2,1,0:T(8,128)(2,1)S(1)}, bf16[2,64,2048]{2,1,0:T(8,128)(2,1)}, u32[]{:S(2)}) copy-start(bf16[2,64,2048]{2,1,0:T(8,128)(2,1)} %param.23) | copy-start | bytes 1572868
  841.5 85.1 %copy-start.12 = (bf16[128,5632]{1,0:T(8,128)(2,1)}, bf16[128,5632]{1,0:T(8,128)(2,1)S(1)}, u32[]{:S(2)}) copy-start(bf16[128,5632]{1,0:T(8,128)(2,1)S(1)} %get-tuple-element.129) | copy-start | bytes 4325380
  866.8 50.6 %copy-start.8 = (f32[128,2048]{1,0:T(8,128)}, f32[128,2048]{1,0:T(8,128)S(1)}, u32[]{:S(2)}) copy-start(f32[128,2048]{1,0:T(8,128)S(1)} %multiply_add_fusion.4) | copy-start | bytes 3145732
  877.1 2436.2 %reduce-scatter.2.cloned.1.call-start = ((), (), s32[]{:S(2)}) async-start(), calls=%async_computation.9 | async-start | bytes 211943424 | tf_op jit(solution)/shard_map/reduce_scatter | solution.py:327
  1182.7 58.3 %copy-start.9 = (f32[128,2048]{1,0:T(8,128)S(1)}, f32[128,2048]{1,0:T(8,128)}, u32[]{:S(2)}) copy-start(f32[128,2048]{1,0:T(8,128)} %copy-done.8) | copy-start | bytes 3145732
  (30 other events, 284.1 us)
Sparse Core Ops, SparseCore 0:
  11.0 159.1 all-gather.10
  201.6 45.3 all-gather.12
  249.1 50.0 all-gather.14
  301.2 45.8 all-gather.22
  350.0 76.1 all-gather.16
  428.9 253.8 all-gather.18
  685.6 142.7 all-gather.20
  877.2 49.4 all-gather.24
  1167.1 2146.1 reduce-scatter.1
where the time goes:
time: 3340 us; the launch traced here: 3330 us
  waiting for transfers between devices  2650 us (79%)
  matrix products  234 us (7%)
  blocking collectives  170 us (5%)
  other arithmetic  161 us (5%)
  local copies, waits for them, and re-layouts  104 us (3%)
    reduce_scatter x1, waiting for transfers between devices, on_device(): lax.psum_scatter(jnp.concatenate([lax.dot_general(left_rows, right_rows,...  2070 us
    all_gather x1, waiting for transfers between devices, on_device(): lax.all_gather(gate_up_weight, ('dp', 'ctx'), axis=0, tiled=True)  246 us
    concatenate x1, other arithmetic, on_device(): jnp.concatenate([lax.dot_general(left_rows, right_rows, (((0,), (0,)), ((...  133 us
    all_gather x1, waiting for transfers between devices, on_device(): lax.all_gather(down_weight, ('dp', 'ctx'), axis=0, tiled=True)  125 us
    unnamed x2, blocking collectives  83.9 us
    dot_general x4, matrix products, on_device(): lax.dot_general(left_rows, right_rows, (((0,), (0,)), ((), ())), preferre...  79.9 us
    all_gather x1, waiting for transfers between devices, on_device(): lax.all_gather(out_weight, ('dp', 'ctx'), axis=0, tiled=True)  72.8 us
    all_gather x1, waiting for transfers between devices, on_device(): weight_piece = lax.all_gather(qkv_weight, ('dp', 'ctx'), axis=0, tiled=True)  69.5 us
  transfers between devices with their start and end apart: 9, of which 8 were waited for; matrix products, arithmetic and copies ran while one was open for 6% of the time, Pallas kernels for 0%

commit v1 on v0

v1 whole, which is shorter than its diff:
```python
import jax
import jax.numpy as jnp
from jax import lax
from jax.experimental import pallas as pl
from jax.experimental.layout import Layout, with_layout_constraint
from jax.experimental.pallas import tpu as pltpu
from jax.sharding import PartitionSpec as P

D = 2048
HEADS = 32
HEAD = 64
ROT = 16
FF = 5632

EPS = 1e-05
LOW = -1e30
F32 = jnp.float32
BF16 = jnp.bfloat16
LANES = 128
VMEM = 56 * 1024 * 1024

def statistics(values):
    average = jnp.mean(values, axis=-1, keepdims=True)
    centred = values - average
    spread = jnp.mean(centred * centred, axis=-1, keepdims=True)
    scaling = lax.rsqrt(spread + EPS)
    return (centred * scaling, scaling)


def norm_back(grad_hat, normal, scaling):
    first = jnp.mean(grad_hat, axis=-1, keepdims=True)
    second = jnp.mean(grad_hat * normal, axis=-1, keepdims=True)
    return scaling * (grad_hat - first - normal * second)


def dot(left, right):
    return jnp.dot(left, right, preferred_element_type=F32)


def dot_t(left, right):
    return lax.dot_general(left, right, (((1,), (1,)), ((), ())), preferred_element_type=F32)


def t_dot(left, right):
    return lax.dot_general(left, right, (((0,), (0,)), ((), ())), preferred_element_type=F32)


def in_rows(value):
    return with_layout_constraint(value, Layout(tuple(range(value.ndim))))


def part(left, right):
    return in_rows(t_dot(left, right).astype(BF16))


def after(value, *earlier):
    if not jax.tree.leaves(earlier):
        return value
    zero = sum(
        lax.slice(one, (0,) * one.ndim, (1,) * one.ndim).reshape(()).astype(F32) * 0.0
        for one in jax.tree.leaves(earlier)
    )
    return value + zero.astype(value.dtype)


def pick(values, index, axis=0):
    return lax.dynamic_index_in_dim(values, index, axis, keepdims=False)


def flip(value, axis, k):
    count = lax.axis_size(axis)
    return lax.ppermute(value, axis, [(i, i ^ k) for i in range(count)])


def place_kernel(sources, splits, *refs):
    step = pl.program_id(0)
    arrays, outs = refs[1 : len(refs) - len(splits)], refs[len(refs) - len(splits) :]
    for i, (which, sub) in enumerate(sources):

        @pl.when(step == i)
        def _(array=arrays[which], sub=sub):
            start = 0
            for out, width in zip(outs, splits):
                out[...] = array[sub, :, start : start + width].reshape(out.shape)
                start += width


def place(sources, at, shape, block, index, splits):
    arrays = []
    for array, _ in sources:
        if not any(array is one for one in arrays):
            arrays.append(array)
    found = [
        (next(n for n, one in enumerate(arrays) if one is array), sub) for array, sub in sources
    ]
    size = sum(array.size for array in arrays)
    return pl.pallas_call(
        lambda *refs: place_kernel(found, splits, *refs),
        out_shape=[jax.ShapeDtypeStruct(shape + (width,), BF16) for width in splits],
        grid_spec=pltpu.PrefetchScalarGridSpec(
            num_scalar_prefetch=1,
            grid=(len(sources),),
            in_specs=[pl.BlockSpec(array.shape, lambda i, at: (0, 0, 0)) for array in arrays],
            out_specs=[pl.BlockSpec(block + (width,), index) for width in splits],
        ),
        compiler_params=pltpu.CompilerParams(vmem_limit_bytes=VMEM),
        cost_estimate=pl.CostEstimate(flops=0, bytes_accessed=4 * size, transcendentals=0),
        name="place",
    )(at, *arrays)


def index_of(*names):
    return jnp.stack([lax.axis_index(name) for name in names]).astype(jnp.int32)


def exchange(blocks):
    return lax.all_to_all(blocks, "ctx", 0, 0, tiled=True)


def halved(value):
    return value.reshape(2, -1, value.shape[-1])


def early_dp(block):
    block = in_rows(halved(block))
    count = lax.axis_size("dp")
    return [flip(block, "dp", k) for k in range(1, 3 if count == 4 else count)]


def late_dp(block, early, *hold):
    sources = [[(piece, 0), (piece, 1)] for piece in [halved(block)] + early]
    if lax.axis_size("dp") != 4:
        return sources
    one, two = early
    first, second = flip(after(one[:1], hold), "dp", 2), flip(after(two[1:], hold), "dp", 1)
    return sources + [[(first, 0), (second, 0)]]


def from_dp(block):
    return late_dp(block, early_dp(block))


def gather_dp(chunks, splits, *hold):
    nd, many = len(chunks[0]), 2 * len(chunks)
    rows = chunks[0][0][0][0].shape[1]
    at = after(index_of("dp"), hold)
    placed = place(
        [half for pieces in zip(*chunks) for piece in pieces for half in piece],
        at,
        (nd, many, rows),
        (1, 1, rows),
        lambda i, at: ((i // many) ^ at[0], i % many, 0, 0),
        splits,
    )
    return [one.reshape(D, one.shape[-1]) for one in placed]


def cross_cores(pieces, other):
    here = {}

    def crossed(half):
        array, sub = half
        if id(array) not in here:
            here[id(array)] = flip(array, "ctx", 1)
        return here[id(array)], sub

    others = [[crossed(half) for half in piece] for piece in pieces[1:]]
    other = halved(other)
    return [[(other, 0), (other, 1)]] + others, list(here.values())


def gather_halves(pieces, others, *hold):
    nd = len(pieces)
    rows, width = pieces[0][0][0].shape[1:]
    (placed,) = place(
        [half for pair in zip(pieces, others) for piece in pair for half in piece],
        after(index_of("dp", "ctx"), hold),
        (2 * nd, 2, rows),
        (1, 1, rows),
        lambda i, at: (2 * ((i // 4) ^ at[0]) + ((i // 2 % 2) ^ (at[1] % 2)), i % 2, 0, 0),
        [width],
    )
    return placed.reshape(D, width)


def sum_dp(parts, *hold):
    nd, nc = lax.axis_size("dp"), lax.axis_size("ctx")
    me = lax.axis_index("dp")
    width = parts.shape[-1]
    parts = parts.astype(BF16).reshape(nd, 2, -1, width)
    if nd != 4:
        total = pick(parts, me).astype(F32)
        for k in range(1, nd):
            total = total + flip(pick(parts, me ^ k), "dp", k).astype(F32)
    else:
        near, one, two, far = (pick(parts, me ^ k) for k in range(4))
        first, second = flip(far[0], "dp", 1), flip(far[1], "dp", 2)
        one_early, two_early = flip(one[0], "dp", 1), flip(two[1], "dp", 2)
        one_late = (one[1].astype(F32) + second.astype(F32)).astype(BF16)
        two_late = (two[0].astype(F32) + first.astype(F32)).astype(BF16)
        one_late = flip(after(one_late, hold), "dp", 1)
        two_late = flip(after(two_late, hold), "dp", 2)
        total = jnp.stack(
            [
                near[0].astype(F32) + one_early.astype(F32) + two_late.astype(F32),
                near[1].astype(F32) + one_late.astype(F32) + two_early.astype(F32),
            ]
        )
    return total.astype(BF16).reshape(nc, -1, width)


def norm_qkv_kernel(x_ref, gain, bias, w_ref, b_ref, cos, up, down, n_ref, hat_ref, qkv_ref):
    hw = cos.shape[1]
    x = x_ref[...].reshape(n_ref.shape[0], x_ref.shape[3])[:, :D].astype(F32)
    average = jnp.mean(x, axis=-1, keepdims=True)
    centred = x - average
    scaling = lax.rsqrt(jnp.mean(centred * centred, axis=-1, keepdims=True) + EPS)
    hat = centred * scaling
    normed = (hat * gain[...] + bias[...]).astype(BF16)
    n_ref[...] = normed
    hat_ref[...] = hat.astype(BF16)
    mixed = dot(normed, w_ref[...]) + b_ref[...]
    for part_at in range(3):
        value = mixed[:, part_at * hw : (part_at + 1) * hw]
        if part_at < 2:
            value = (
                value * cos[...]
                + pltpu.roll(value, hw - ROT // 2, 1) * up[...]
                + pltpu.roll(value, ROT // 2, 1) * down[...]
            )
        qkv_ref[:, part_at * hw : (part_at + 1) * hw] = value.astype(BF16)


def norm_qkv(x_ext, gain, bias, w_qkv, b_qkv, tables, length):
    nc, seqs, span, wide = x_ext.shape
    tokens = seqs * length
    cols = w_qkv.shape[1]
    step = min(512, length)
    per = length // step

    def whole(array):
        return pl.BlockSpec(array.shape, lambda i: (0, 0))

    return pl.pallas_call(
        norm_qkv_kernel,
        out_shape=[
            jax.ShapeDtypeStruct((tokens, D), BF16),
            jax.ShapeDtypeStruct((tokens, D), BF16),
            jax.ShapeDtypeStruct((tokens, cols), BF16),
        ],
        grid=(tokens // step,),
        in_specs=[
            pl.BlockSpec((step // span, 1, span, wide), lambda i: (i % per, i // per, 0, 0)),
            whole(gain),
            whole(bias),
            whole(w_qkv),
            whole(b_qkv),
        ]
        + [pl.BlockSpec((step, cols // 3), lambda i: (i % per, 0))] * 3,
        out_specs=[
            pl.BlockSpec((step, D), lambda i: (i, 0)),
            pl.BlockSpec((step, D), lambda i: (i, 0)),
            pl.BlockSpec((step, cols), lambda i: (i, 0)),
        ],
        compiler_params=pltpu.CompilerParams(vmem_limit_bytes=VMEM),
        cost_estimate=pl.CostEstimate(
            flops=2 * tokens * D * cols,
            bytes_accessed=4 * tokens * D + 2 * D * cols + 2 * tokens * cols,
            transcendentals=0,
        ),
        name="norm_qkv",
    )(x_ext, gain, bias, w_qkv, b_qkv, *tables)


def seen(seg_col, seg_row):
    shape = (seg_col.shape[1], seg_row.shape[2])
    query = lax.broadcasted_iota(jnp.int32, shape, 0)
    key = lax.broadcasted_iota(jnp.int32, shape, 1)
    return (key <= query) & (seg_col[0] == seg_row[0])


def attend_kernel(mine, qkv_ref, seg_col, seg_row, a_ref, log_ref):
    hw = mine * HEAD
    allowed = seen(seg_col, seg_row)
    lane = lax.broadcasted_iota(jnp.int32, log_ref.shape[1:], 1)
    logs = jnp.zeros(log_ref.shape[1:], F32)
    for head in range(mine):
        q, k, v = (
            qkv_ref[0, :, at * hw + head * HEAD : at * hw + (head + 1) * HEAD] for at in range(3)
        )
        scores = jnp.where(allowed, dot_t(q, k) * HEAD**-0.5, LOW)
        peak = jnp.max(scores, axis=-1, keepdims=True)
        weights = jnp.exp(scores - peak)
        total = jnp.sum(weights, axis=-1, keepdims=True)
        out = dot(weights.astype(BF16), v) / total
        a_ref[0, :, head * HEAD : (head + 1) * HEAD] = out.astype(BF16)
        logs = jnp.where(lane == head, peak + jnp.log(total), logs)
    log_ref[0] = logs


def attend(qkv, seg_col, seg_row, mine):
    seqs, length, cols = qkv.shape
    hw = cols // 3
    return pl.pallas_call(
        lambda *refs: attend_kernel(mine, *refs),
        out_shape=[
            jax.ShapeDtypeStruct((seqs, length, hw), BF16),
            jax.ShapeDtypeStruct((seqs, length, LANES), F32),
        ],
        grid=(seqs,),
        in_specs=[
            pl.BlockSpec((1, length, cols), lambda s: (s, 0, 0)),
            pl.BlockSpec((1, length, 1), lambda s: (s, 0, 0)),
            pl.BlockSpec((1, 1, length), lambda s: (s, 0, 0)),
        ],
        out_specs=[
            pl.BlockSpec((1, length, hw), lambda s: (s, 0, 0)),
            pl.BlockSpec((1, length, LANES), lambda s: (s, 0, 0)),
        ],
        compiler_params=pltpu.CompilerParams(vmem_limit_bytes=VMEM),
        cost_estimate=pl.CostEstimate(
            flops=4 * seqs * length * length * hw,
            bytes_accessed=8 * seqs * length * hw,
            transcendentals=seqs * mine * length * length,
        ),
        name="attend",
    )(qkv, seg_col, seg_row)


def attend_back_kernel(
    mine, qkv_ref, do_ref, log_ref, seg_col, seg_row, cos, up, down, dm_ref, dq_all, dk_all
):
    hw = mine * HEAD
    allowed = seen(seg_col, seg_row)
    for head in range(mine):
        at_head = slice(head * HEAD, (head + 1) * HEAD)
        q, k, v = (
            qkv_ref[0, :, at * hw + head * HEAD : at * hw + (head + 1) * HEAD] for at in range(3)
        )
        do = do_ref[0, :, at_head]
        log_total = log_ref[0, :, head : head + 1]
        p = jnp.where(allowed, jnp.exp(dot_t(q, k) * HEAD**-0.5 - log_total), 0.0)
        push = dot_t(do, v)
        delta = jnp.sum(p * push, axis=-1, keepdims=True)
        ds = (p * (push - delta) * HEAD**-0.5).astype(BF16)
        dq_all[:, at_head] = dot(ds, k)
        dk_all[:, at_head] = t_dot(ds, q)
        start = 2 * hw + head * HEAD
        dm_ref[0, :, start : start + HEAD] = t_dot(p.astype(BF16), do).astype(BF16)
    for at, held in enumerate((dq_all, dk_all)):
        value = held[...]
        value = (
            value * cos[...]
            - pltpu.roll(value, hw - ROT // 2, 1) * up[...]
            - pltpu.roll(value, ROT // 2, 1) * down[...]
        )
        dm_ref[0, :, at * hw : (at + 1) * hw] = value.astype(BF16)


def attend_back(qkv, do, logs, seg_col, seg_row, tables, mine):
    seqs, length, cols = qkv.shape
    hw = cols // 3

    def of_sequence(array):
        return pl.BlockSpec((1,) + array.shape[1:], lambda s: (s, 0, 0))

    return pl.pallas_call(
        lambda *refs: attend_back_kernel(mine, *refs),
        out_shape=jax.ShapeDtypeStruct((seqs, length, cols), BF16),
        grid=(seqs,),
        in_specs=[of_sequence(array) for array in (qkv, do, logs, seg_col, seg_row)]
        + [pl.BlockSpec((length, hw), lambda s: (0, 0))] * 3,
        out_specs=pl.BlockSpec((1, length, cols), lambda s: (s, 0, 0)),
        scratch_shapes=[pltpu.VMEM((length, hw), F32)] * 2,
        compiler_params=pltpu.CompilerParams(vmem_limit_bytes=VMEM),
        cost_estimate=pl.CostEstimate(
            flops=10 * seqs * length * length * hw,
            bytes_accessed=20 * seqs * length * hw,
            transcendentals=seqs * mine * length * length,
        ),
        name="attend_back",
    )(qkv, do, logs, seg_col, seg_row, *tables)


def out_norm_kernel(span, per, a_ref, w_ref, x_ref, gain, bias, at, n_ref, own_ref, held):
    block = pl.program_id(0)
    x = x_ref[...].reshape(a_ref.shape[0], x_ref.shape[3])[:, :D].astype(F32)
    h1 = x + dot(a_ref[...], w_ref[...])
    average = jnp.mean(h1, axis=-1, keepdims=True)
    centred = h1 - average
    scaling = lax.rsqrt(jnp.mean(centred * centred, axis=-1, keepdims=True) + EPS)
    n_ref[...] = (centred * scaling * gain[...] + bias[...]).astype(BF16)
    held[...] = h1
    spans = a_ref.shape[0] // span

    @pl.when(block % per == at[0] // spans)
    def _():
        start = pl.multiple_of((at[0] % spans) * span, span)
        own_ref[0] = held[pl.ds(start, span), :]


def out_norm(a_all, w_out, x_ext, gain, bias, at):
    nc, seqs, span, wide = x_ext.shape
    length = nc * span
    tokens = seqs * length
    step = min(512, length)
    per = length // step
    return pl.pallas_call(
        lambda at, a, w, x, gain, bias, n, own, held: out_norm_kernel(
            span, per, a, w, x, gain, bias, at, n, own, held
        ),
        out_shape=[
            jax.ShapeDtypeStruct((tokens, D), BF16),
            jax.ShapeDtypeStruct((seqs, span, D), F32),
        ],
        grid_spec=pltpu.PrefetchScalarGridSpec(
            num_scalar_prefetch=1,
            grid=(tokens // step,),
            in_specs=[
                pl.BlockSpec((step, D), lambda i, at: (i, 0)),
                pl.BlockSpec((D, D), lambda i, at: (0, 0)),
                pl.BlockSpec(
                    (step // span, 1, span, wide), lambda i, at: (i % per, i // per, 0, 0)
                ),
                pl.BlockSpec((1, D), lambda i, at: (0, 0)),
                pl.BlockSpec((1, D), lambda i, at: (0, 0)),
            ],
            out_specs=[
                pl.BlockSpec((step, D), lambda i, at: (i, 0)),
                pl.BlockSpec((1, span, D), lambda i, at: (i // per, 0, 0)),
            ],
            scratch_shapes=[pltpu.VMEM((step, D), F32)],
        ),
        compiler_params=pltpu.CompilerParams(vmem_limit_bytes=VMEM),
        cost_estimate=pl.CostEstimate(
            flops=2 * tokens * D * D, bytes_accessed=6 * tokens * D + 2 * D * D, transcendentals=0
        ),
        name="out_norm",
    )(at, a_all, w_out, x_ext, gain, bias)


def widen_kernel(hw, blocks_ref, qkv_ref, out_ref):
    step = pl.program_id(0)
    value = [blocks_ref[c].astype(F32) for c in range(blocks_ref.shape[0])]

    @pl.when(step < 3)
    def _():
        for c, one in enumerate(value):
            qkv_ref[:, c * hw : (c + 1) * hw] = one

    @pl.when(step == 3)
    def _():
        for c, one in enumerate(value):
            out_ref[:, c * hw : (c + 1) * hw] = one


def widen(blocks, hw):
    nc, rows, _ = blocks.shape
    return pl.pallas_call(
        lambda *refs: widen_kernel(hw, *refs),
        out_shape=[
            jax.ShapeDtypeStruct((rows, 3 * D), F32),
            jax.ShapeDtypeStruct((rows, D), F32),
        ],
        grid=(4,),
        in_specs=[pl.BlockSpec((nc, rows, hw), lambda j: (0, 0, j))],
        out_specs=[
            pl.BlockSpec((rows, D), lambda j: (0, jnp.minimum(j, 2))),
            pl.BlockSpec((rows, D), lambda j: (0, 0)),
        ],
        compiler_params=pltpu.CompilerParams(vmem_limit_bytes=VMEM),
        cost_estimate=pl.CostEstimate(
            flops=0, bytes_accessed=24 * rows * D, transcendentals=0
        ),
        name="widen",
    )(blocks)


def on_device(
    hidden_in,
    segment_ids,
    norm1_gain,
    norm1_bias,
    qkv_weight,
    qkv_bias,
    out_weight,
    norm2_gain,
    norm2_bias,
    gate_up_weight,
    down_weight,
    out_grad,
):
    nc = lax.axis_size("ctx")
    me = lax.axis_index("ctx")
    seqs, span, _ = hidden_in.shape
    own_tokens = seqs * span
    length = nc * span
    tokens = seqs * length
    rows = qkv_weight.shape[0]
    mine = HEADS // nc
    hw = mine * HEAD
    fw = FF // nc

    def gather_tokens(values):
        return lax.all_gather(values, "ctx", axis=1, tiled=True)

    def scatter_tokens(partial):
        partial = partial.reshape(seqs, length, D)
        return lax.psum_scatter(partial, "ctx", scatter_dimension=1, tiled=True).reshape(
            own_tokens, D
        )

    vectors = [norm1_gain, norm1_bias, norm2_gain, norm2_bias]
    extra = jnp.concatenate([jnp.stack(vectors, axis=1), qkv_bias.reshape(rows, 3)], axis=1)
    extra = jnp.pad(extra, ((0, 0), (0, LANES - 7)))
    blocks = qkv_weight.reshape(rows, 3, nc, hw).transpose(2, 0, 1, 3).reshape(nc, rows, 3 * hw)
    blocks = jnp.concatenate(
        [blocks, jnp.broadcast_to(extra[None], (nc, rows, LANES))], axis=2
    )
    qkv_block = exchange(blocks)

    seg = jnp.pad(segment_ids.astype(BF16)[..., None], ((0, 0), (0, 0), (0, LANES - 1)))
    x_ext = jnp.concatenate([hidden_in, seg], axis=2)
    out_block = lax.all_gather(out_weight, "ctx", axis=0, tiled=True)
    gu_t = gate_up_weight.reshape(rows, 2, nc, fw).transpose(2, 0, 1, 3).reshape(nc, rows, 2 * fw)
    down_t = down_weight.reshape(rows, nc, fw).transpose(1, 0, 2)
    gu_t, down_t = lax.optimization_barrier(gu_t), lax.optimization_barrier(down_t)
    places = jnp.arange(length, dtype=jnp.int32)
    frequency = 10000.0 ** (-jnp.arange(ROT // 2).astype(F32) * 2.0 / ROT)
    angles = places.astype(F32)[:, None] * frequency[None, :]
    cosine, sine = jnp.cos(angles), jnp.sin(angles)
    half = jnp.zeros_like(sine)
    rest = jnp.zeros((length, HEAD - ROT), F32)
    tables = [
        lax.optimization_barrier(in_rows(jnp.tile(jnp.concatenate(columns, axis=1), (1, mine))))
        for columns in (
            (cosine, cosine, rest + 1.0),
            (-sine, half, rest),
            (half, sine, rest),
        )
    ]
    x_ext = after(x_ext, qkv_block, out_block, gu_t, down_t, tables)
    x_ext = lax.all_gather(x_ext, "ctx", axis=0, tiled=False)
    seg = x_ext[:, :, :, D].transpose(1, 0, 2).reshape(seqs, length).astype(F32)
    seg_col, seg_row = seg[:, :, None], seg[:, None, :]

    qkv_pieces = from_dp(qkv_block)
    out_halves = halved(out_block)
    there = [half[0] for piece in qkv_pieces for half in piece]
    out_block = after(pick(out_halves, me % 2), there)

    w_qkv, extra = gather_dp([qkv_pieces], [3 * hw, LANES])
    extra = extra[:, :7].astype(F32)
    gain_one, bias_one, gain_two, bias_two = (extra[:, i][None] for i in range(4))
    b_qkv = pick(extra[:, 4:].reshape(3, nc, hw), me, 1).reshape(1, 3 * hw)

    gu_block = exchange(after(gu_t, x_ext, w_qkv, gain_one, b_qkv))
    down_block = exchange(after(down_t, gu_block))
    gu_halves = gu_block.reshape(2, -1, 2 * fw)

    out_early = early_dp(out_block)
    n1, hat_all, qkv = norm_qkv(x_ext, gain_one, bias_one, w_qkv, b_qkv, tables, length)
    qkv = qkv.reshape(seqs, length, 3 * hw)
    a_mine, logs = attend(qkv, seg_col, seg_row, mine)
    out_pieces = late_dp(out_block, out_early, logs)
    out_others, _ = cross_cores(out_pieces, pick(out_halves, 1 - me % 2))
    w_out = gather_halves(out_pieces, out_others, logs)
    gu_early = early_dp(after(gu_halves[0], out_early))
    gu_early_two = early_dp(after(gu_halves[1], gu_early))
    down_early = early_dp(after(down_block, gu_early_two))
    a_mine = after(a_mine, w_out, gu_early, down_block)
    a_all = lax.all_gather(a_mine, "ctx", axis=2, tiled=True).reshape(tokens, D)
    dy = gather_tokens(after(out_grad, a_all, gu_early_two, down_early)).reshape(tokens, D)

    at = me.astype(jnp.int32).reshape(1)
    n2, h1 = out_norm(a_all, w_out, x_ext, gain_two, bias_two, at)
    h1 = h1.reshape(own_tokens, D)
    gu_pieces = [late_dp(gu_halves[0], gu_early), late_dp(gu_halves[1], gu_early_two)]
    (w_gu,) = gather_dp(gu_pieces, [2 * fw], n2)
    gu = dot(n2, w_gu)
    (w_down,) = gather_dp([late_dp(down_block, down_early)], [fw], gu)
    gate = gu[:, :fw]
    up = gu[:, fw:]
    sg = jax.nn.sigmoid(gate)
    hid = (gate * sg * up).astype(BF16)
    branch_part = dot_t(hid, w_down).astype(BF16)

    dhid = dot(dy, w_down)
    dgate = (dhid * up * sg * (1.0 + gate * (1.0 - sg))).astype(BF16)
    dup = (dhid * gate * sg).astype(BF16)
    dgu = jnp.concatenate([dgate, dup], axis=1)
    dn2 = scatter_tokens(dot_t(dgu, w_gu).astype(BF16))
    down_part = part(dy, hid)
    gate_part = part(n2, dgate)
    up_part = part(n2, dup)
    down_sum = sum_dp(down_part)
    dn2 = after(dn2, down_sum, gate_part, up_part, branch_part)
    gate_sum = sum_dp(gate_part, dn2)
    branch = scatter_tokens(after(branch_part, dn2))
    dn2 = dn2.astype(F32)
    hat_two, scale_two = statistics(h1)
    gain_two_grad = jnp.sum(dn2 * hat_two, axis=0)
    bias_two_grad = jnp.sum(dn2, axis=0)
    dh1 = out_grad.reshape(own_tokens, D).astype(F32) + norm_back(dn2 * gain_two, hat_two, scale_two)
    dp1 = dh1.astype(BF16)
    do = dot_t(dp1, w_out).astype(BF16)
    pairs = jnp.stack([do, dp1], axis=0).reshape(2, seqs, span, nc, hw)
    pairs = exchange(pairs.transpose(3, 0, 1, 2, 4).reshape(nc, 2 * own_tokens, hw))
    pairs = pairs.reshape(nc, 2, seqs, span, hw).transpose(1, 2, 0, 3, 4)
    do = pairs[0].reshape(seqs, length, hw)
    dp1_mine = pairs[1].reshape(tokens, hw)

    do = after(do, gate_sum)
    early_blocks = exchange(after(jnp.concatenate([gate_sum, down_sum], axis=2), do))

    dm1 = attend_back(qkv, do, logs, seg_col, seg_row, tables, mine).reshape(tokens, 3 * hw)
    up_sum = sum_dp(up_part, dm1)
    late_blocks = exchange(up_sum)
    qkv_part = part(n1, dm1)
    a_part = part(a_all, dp1_mine)
    qkv_sum = sum_dp(qkv_part, a_part)
    dn1_part = dot_t(dm1, w_qkv)
    dn1 = scatter_tokens(after(dn1_part.astype(BF16), qkv_part, early_blocks, up_sum, branch))
    bias_part = jnp.sum(dm1.astype(F32), axis=0).reshape(3, 1, hw)
    bias_full = lax.dynamic_update_slice_in_dim(jnp.zeros((3, nc, hw), F32), bias_part, me, 1)
    small = jnp.concatenate(
        [
            jnp.stack(
                [
                    jnp.sum(dn1_part * hat_all.astype(F32), axis=0),
                    jnp.sum(dn1_part, axis=0),
                    gain_two_grad,
                    bias_two_grad,
                ],
                axis=1,
            ),
            bias_full.reshape(D, 3),
        ],
        axis=1,
    )
    small = jnp.pad(small, ((0, 0), (0, LANES - 7)))
    small = small.astype(BF16)
    out_part = jnp.concatenate([a_part, small], axis=1)
    parts = jnp.concatenate([qkv_sum, sum_dp(out_part)], axis=2)
    dn1 = after(dn1, parts, late_blocks)
    def spread(blocks):
        return blocks.transpose(1, 0, 2).reshape(rows, FF).astype(F32)

    gate_grad, down_grad = spread(early_blocks[:, :, :fw]), spread(early_blocks[:, :, fw:])
    up_grad = spread(late_blocks)
    dn1 = dn1.astype(F32)
    result = (h1 + branch.astype(F32)).astype(BF16).reshape(seqs, span, D)
    hat_one, scale_one = statistics(hidden_in.reshape(own_tokens, D).astype(F32))
    dx = dh1 + norm_back(dn1 * gain_one, hat_one, scale_one)
    grad_result = dx.astype(BF16).reshape(seqs, span, D)

    blocks = exchange(parts)
    qkv_grad, out_grad_w = widen(blocks, hw)
    sums = jnp.sum(blocks[:, :, 4 * hw : 4 * hw + 7].astype(F32), axis=0)
    return (
        result,
        grad_result,
        sums[:, 0],
        sums[:, 1],
        qkv_grad,
        sums[:, 4:].reshape(3 * rows),
        out_grad_w,
        sums[:, 2],
        sums[:, 3],
        jnp.concatenate([gate_grad, up_grad], axis=1),
        down_grad,
    )


def solution(mesh):
    token = P("dp", "ctx", None)
    vector = P(("dp", "ctx"))
    matrix = P(("dp", "ctx"), None)
    return jax.shard_map(
        on_device,
        mesh=mesh,
        in_specs=(
            token,
            P("dp", "ctx"),
            vector,
            vector,
            matrix,
            vector,
            matrix,
            vector,
            vector,
            matrix,
            matrix,
            token,
        ),
        out_specs=(
            token,
            token,
            vector,
            vector,
            matrix,
            vector,
            matrix,
            vector,
            vector,
            matrix,
            matrix,
        ),
        check_vma=False,
    )
```

time: 3340 us -> 654 us (0.20)
  waiting for transfers between devices: 2650 us -> 185 us
  blocking collectives: 170 us -> 0 us
  matrix products: 234 us -> 74.9 us
  other arithmetic: 161 us -> 53.7 us
  Pallas kernels: 0 us -> 84.8 us
  starting transfers between devices: 0.88 us -> 84.9 us
    reduce_scatter x1 -> x3, waiting for transfers between devices: 2070 us -> 1.89 us  [scatter_tokens(): lax.psum_scatter(partial, 'ctx', scatter_dimension=1, tiled=True)]
    all_gather x8 -> x4, waiting for transfers between devices: 574 us -> 0.05 us  [the longest x1 0.02 us: on_device(): a_all = lax.all_gather(a_mine, 'ctx', axis=2, tiled=True).reshape(tokens, D)]
    dot_general x18 -> x11, matrix products: 234 us -> 74.9 us  [the longest x4 29.3 us: dot_t(): lax.dot_general(left, right, (((1,), (1,)), ((), ())), preferred_element_...]
    ppermute x0 -> x54, waiting for transfers between devices: none -> 134 us  [flip(): return lax.ppermute(value, axis, [(i, i ^ k) for i in range(count)])]
    concatenate x1 -> x5, other arithmetic: 133 us -> 7.58 us  [the longest x1 2.87 us: on_device(): jnp.concatenate([gate_grad, up_grad], axis=1)]
    all_gather x4 -> x0, blocking collectives: 86.5 us -> none  [the longest x1 40.7 us: on_device(): lax.all_gather(qkv_bias.reshape(own_rows, 3), ('dp', 'ctx'), axis=0, tile...]
    pallas_call x0 -> x9, Pallas kernels: none -> 84.8 us  [the longest x4 31.7 us: place(): pl.pallas_call(lambda *refs: place_kernel(found, splits, *refs), out_shap...]
    unnamed x2 -> x0, blocking collectives: 83.9 us -> none
  transfers between devices with their start and end apart: 9 -> 68, of which waited for: 8 -> 29; matrix products, arithmetic and copies ran while one was open for 6% -> 28% of each run, Pallas kernels for 0% -> 13%
where the time goes in v1:
time: 654 us; the launch traced here: 644 us
  waiting for transfers between devices  185 us (28%)
  local copies, waits for them, and re-layouts  114 us (17%)
  starting transfers between devices  84.9 us (13%)
  Pallas kernels  84.8 us (13%)
  matrix products  74.9 us (11%)
  other arithmetic  53.7 us (8%)
  between operations  46.8 us (7%)
    ppermute x54, waiting for transfers between devices, flip(): return lax.ppermute(value, axis, [(i, i ^ k) for i in range(count)])  134 us
    ppermute x54, starting transfers between devices, flip(): return lax.ppermute(value, axis, [(i, i ^ k) for i in range(count)])  54.5 us
    all_to_all x7, waiting for transfers between devices, exchange(): return lax.all_to_all(blocks, 'ctx', 0, 0, tiled=True)  48.8 us
    slice x46, local copies, waits for them, and re-layouts, after(): lax.slice(one, (0,) * one.ndim, (1,) * one.ndim).reshape(()).astype(F32)  38.1 us
    pallas_call x4, Pallas kernels, place(): pl.pallas_call(lambda *refs: place_kernel(found, splits, *refs), out_shap...  31.7 us
    all_to_all x7, starting transfers between devices, exchange(): return lax.all_to_all(blocks, 'ctx', 0, 0, tiled=True)  30.2 us
    dot_general x4, matrix products, dot_t(): lax.dot_general(left, right, (((1,), (1,)), ((), ())), preferred_element_...  29.3 us
    dot_general x5, matrix products, t_dot(): lax.dot_general(left, right, (((0,), (0,)), ((), ())), preferred_element_...  24.8 us
  transfers between devices with their start and end apart: 68, of which 29 were waited for; matrix products, arithmetic and copies ran while one was open for 28% of the time, Pallas kernels for 13%

profile of v1, /device:TPU:0, one launch (start us, length us, event | category | flops | bytes accessed | tf_op | source)
XLA Modules:
  0.0 644.4 jit_solution(9859149706633749630)
XLA Ops:
  12.1 6.3 all-to-all-start
  38.7 20.5 %all-to-all-done = bf16[8,64,896]{2,1,0:T(8,128)(2,1)} async-done(((bf16[8,64,896]{2,1,0:T(8,128)(2,1)}), bf16[8,64,896]{2,1,0:T(8,128)(2,1)}, u32[]{:S(2)}, u32[]{:S(2)}) %all-to-all-start) | async-done | bytes 917536 | tf_op jit(solution)/shard_map/all_to_all | solution.py:117
  66.9 19.0 %collective-permute-done.refs_2_ = bf16[2,256,896]{2,1,0:T(8,128)(2,1)S(1)} collective-permute-done((bf16[2,256,896]{2,1,0:T(8,128)(2,1)}, bf16[2,256,896]{2,1,0:T(8,128)(2,1)S(1)}, u32[]{:S(2)}, u32[]{:S(2)}) %collective-permute-start) | collective-permute-done | bytes 917536 | tf_op jit(solution)/shard_map/ppermute | solution.py:72
  128.5 13.8 %collective-permute-done.4.refs_3_ = bf16[2,128,2048]{2,1,0:T(8,128)(2,1)} collective-permute-done((bf16[2,128,2048]{2,1,0:T(8,128)(2,1)S(1)}, bf16[2,128,2048]{2,1,0:T(8,128)(2,1)}, u32[]{:S(2)}, u32[]{:S(2)}) %collective-permute-start.4) | collective-permute-done | bytes 1048608 | tf_op jit(solution)/shard_map/ppermute | solution.py:72
  148.8 11.0 %norm_qkv.1 = (bf16[1024,2048]{1,0:T(8,128)(2,1)}, bf16[1024,2048]{1,0:T(8,128)(2,1)}, bf16[1024,768]{1,0:T(8,128)(2,1)}) custom-call(bf16[8,2,64,2176]{3,2,1,0:T(8,128)(2,1)} %all-gather.7.cloned.1.call-done.x_ref.x, f32[1,2048]{1,0:T(1,128)} %copy-done.56, f32[1,2048]{1,0:T(1,128)} %get-tuple-element.99.bias, bf16[2048,768]{1,0:T(8,128)(2,1)} %bitcast.433, ...), custom_call_target="tpu_custom_call" | custom-call | flops 3221225472 | bytes 13107200 | tf_op jit(solution)/shard_map/norm_qkv/pallas_call | solution.py:244
  159.8 8.3 %attend.1 = (bf16[2,512,256]{2,1,0:T(8,128)(2,1)}, f32[2,512,128]{2,1,0:T(8,128)}) custom-call(bf16[2,512,768]{2,1,0:T(8,128)(2,1)} %bitcast.410, f32[2,512,1]{2,1,0:T(8,128)} %reshape.1002.refs_1_.refs_3_, f32[2,1,512]{2,1,0:T(1,128)} %reshape.976.refs_2_.refs_4_), custom_call_target="tpu_custom_call" | custom-call | flops 536870912 | bytes 2097152 | tf_op jit(solution)/shard_map/attend/pallas_call | solution.py:304
  193.2 11.6 %place.5 = bf16[8,2,128,2048]{3,2,1,0:T(8,128)(2,1)} custom-call(s32[2]{0:T(128)} %add_add_fusion.refs_0_, bf16[2,128,2048]{2,1,0:T(8,128)(2,1)} %bitcast.365, bf16[2,128,2048]{2,1,0:T(8,128)(2,1)} %bitcast.362, bf16[2,128,2048]{2,1,0:T(8,128)(2,1)} %collective-permute-done.4.refs_3_, bf16[2,128,2048]{2,1,0:T(8,128)(2,1)} %collective-permute-done.5.refs_4_, ...), custom_call_target="tpu_custom_call" | custom-call | bytes 16777216 | tf_op jit(solution)/shard_map/place/pallas_call | solution.py:97
  214.1 17.2 %collective-permute-done.14.refs_4_ = bf16[2,128,1408]{2,1,0:T(8,128)(2,1)S(1)} collective-permute-done((bf16[2,128,1408]{2,1,0:T(8,128)(2,1)S(1)}, bf16[2,128,1408]{2,1,0:T(8,128)(2,1)S(1)}, u32[]{:S(2)}, u32[]{:S(2)}) %collective-permute-start.14) | collective-permute-done | bytes 720928 | tf_op jit(solution)/shard_map/ppermute | solution.py:72
  237.6 16.7 %collective-permute-done.20 = bf16[2,256,704]{1,2,0:T(8,128)(2,1)} collective-permute-done((bf16[2,256,704]{1,2,0:T(8,128)(2,1)}, bf16[2,256,704]{1,2,0:T(8,128)(2,1)}, u32[]{:S(2)}, u32[]{:S(2)}) %collective-permute-start.20) | collective-permute-done | bytes 720928 | tf_op jit(solution)/shard_map/ppermute | solution.py:72
  271.4 18.0 %out_norm.1 = (bf16[1024,2048]{1,0:T(8,128)(2,1)}, f32[2,64,2048]{2,1,0:T(8,128)}) custom-call(s32[1]{0:T(128)} %bitcast.at, bf16[1024,2048]{1,0:T(8,128)(2,1)} %bitcast.428, bf16[2048,2048]{1,0:T(8,128)(2,1)} %bitcast.338, bf16[8,2,64,2176]{3,2,1,0:T(8,128)(2,1)} %all-gather.7.cloned.1.call-done.x_ref.x, f32[1,2048]{1,0:T(1,128)} %get-tuple-element.98.gain, ...), custom_call_target="tpu_custom_call" | custom-call | flops 8589934592 | bytes 20971520 | tf_op jit(solution)/shard_map/out_norm/pallas_call | solution.py:408
  293.7 9.3 %place.6 = bf16[4,4,128,1408]{3,2,1,0:T(8,128)(2,1)} custom-call(s32[1]{0:T(128)S(6)} %add.532.refs_0_, bf16[2,128,1408]{2,1,0:T(8,128)(2,1)} %bitcast.349, bf16[2,128,1408]{2,1,0:T(8,128)(2,1)} %bitcast.347, bf16[2,128,1408]{2,1,0:T(8,128)(2,1)} %copy-done.36, bf16[2,128,1408]{2,1,0:T(8,128)(2,1)} %copy-done.39, bf16[2,128,1408]{2,1,0:T(8,128)(2,1)} %copy-done.37, ...), custom_call_target="tpu_custom_call" | custom-call | bytes 11534336 | tf_op jit(solution)/shard_map/place/pallas_call | solution.py:97
  303.1 10.5 %fusion.70 = f32[1024,1408]{1,0:T(8,128)S(1)} fusion(bf16[1024,2048]{1,0:T(8,128)(2,1)} %get-tuple-element.28, bf16[2048,1408]{1,0:T(8,128)(2,1)} %bitcast.358), kind=kOutput, calls=%fused_computation.217 | convolution fusion | flops 5905580032 | bytes 15728640 | tf_op jit(solution)/shard_map/dot_general | solution.py:37
  322.1 10.4 %multiply_convert_fusion.1 = (bf16[1024,704]{1,0:T(8,128)(2,1)S(1)}, bf16[1024,704]{1,0:T(8,128)(2,1)S(1)}, bf16[1024,704]{1,0:T(8,128)(2,1)}) fusion(f32[1024,1408]{1,0:T(8,128)} %copy-done.64, bf16[1024,2048]{1,0:T(8,128)(2,1)} %bitcast.430, bf16[2048,704]{1,0:T(8,128)(2,1)} %bitcast.375), kind=kOutput, calls=%fused_computation.11 | convolution fusion | flops 2964324352 | bytes 17170432 | tf_op jit(solution)/shard_map/dot_general | solution.py:37
  332.5 8.6 %convolution_convert_fusion = bf16[1024,2048]{1,0:T(8,128)(2,1)} fusion(bf16[2048,1408]{1,0:T(8,128)(2,1)S(1)} %bitcast.361, bf16[1024,704]{1,0:T(8,128)(2,1)S(1)} %get-tuple-element.47, bf16[1024,704]{1,0:T(8,128)(2,1)S(1)} %get-tuple-element.46), kind=kOutput, calls=%fused_computation.2 | convolution fusion | flops 5913444352 | bytes 12845056 | tf_op jit(solution)/shard_map/dot_general | solution.py:41
  366.7 8.2 %collective-permute-done.26 = bf16[256,704]{1,0:T(8,128)(2,1)S(1)} collective-permute-done((bf16[256,704]{1,0:T(8,128)(2,1)S(1)}, bf16[256,704]{1,0:T(8,128)(2,1)S(1)}, u32[]{:S(2)}, u32[]{:S(2)}) %collective-permute-start.26) | collective-permute-done | bytes 360480 | tf_op jit(solution)/shard_map/ppermute | solution.py:72
  399.9 6.7 %convolution_convert_fusion.7 = bf16[128,2048]{1,0:T(8,128)(2,1)S(1)} fusion(bf16[128,2048]{1,0:T(8,128)(2,1)S(1)} %bitcast.400, bf16[2048,2048]{1,0:T(8,128)(2,1)} %bitcast.339), kind=kOutput, calls=%fused_computation.19 | convolution fusion | flops 1074003968 | bytes 9437184 | tf_op jit(solution)/shard_map/dot_general | solution.py:41
  418.3 7.9 %collective-permute-done.31 = bf16[256,704]{1,0:T(8,128)(2,1)S(1)} collective-permute-done((bf16[256,704]{1,0:T(8,128)(2,1)S(1)}, bf16[256,704]{1,0:T(8,128)(2,1)S(1)}, u32[]{:S(2)}, u32[]{:S(2)}) %collective-permute-start.31) | collective-permute-done | bytes 360480 | tf_op jit(solution)/shard_map/ppermute | solution.py:72
  436.1 7.6 %collective-permute-done.32 = bf16[256,704]{1,0:T(8,128)(2,1)S(1)} collective-permute-done((bf16[256,704]{1,0:T(8,128)(2,1)S(1)}, bf16[256,704]{1,0:T(8,128)(2,1)S(1)}, u32[]{:S(2)}, u32[]{:S(2)}) %collective-permute-start.32) | collective-permute-done | bytes 360480 | tf_op jit(solution)/shard_map/ppermute | solution.py:72
  445.6 10.8 %all-to-all-done.3 = bf16[8,256,256]{2,1,0:T(8,128)(2,1)S(1)} async-done(((bf16[8,256,256]{2,1,0:T(8,128)(2,1)}), bf16[8,256,256]{2,1,0:T(8,128)(2,1)S(1)}, u32[]{:S(2)}, u32[]{:S(2)}) %all-to-all-start.3) | async-done | bytes 1048608 | tf_op jit(solution)/shard_map/all_to_all | solution.py:117
  470.8 12.1 %attend_back.1 = bf16[2,512,768]{2,1,0:T(8,128)(2,1)} custom-call(bf16[2,512,768]{2,1,0:T(8,128)(2,1)} %bitcast.411, bf16[2,512,256]{2,1,0:T(8,128)(2,1)} %bitcast.408, f32[2,512,128]{2,1,0:T(8,128)} %get-tuple-element.26.refs_2_, f32[2,512,1]{2,1,0:T(8,128)} %reshape.1002.refs_1_.refs_3_, f32[2,1,512]{2,1,0:T(1,128)} %reshape.976.refs_2_.refs_4_, ...), custom_call_target="tpu_custom_call" | custom-call | flops 1342177280 | bytes 5242880 | tf_op jit(solution)/shard_map/attend_back/pallas_call | solution.py:367
  503.3 10.4 %convert_add_fusion = (bf16[1024,2048]{1,0:T(8,128)(2,1)}, f32[1024,2048]{1,0:T(8,128)}) fusion(bf16[]{:T(256)S(6)} %add.597, bf16[1024,768]{1,0:T(8,128)(2,1)} %bitcast.357, bf16[2048,768]{1,0:T(8,128)(2,1)} %bitcast.434), kind=kOutput, calls=%fused_computation.1 | convolution fusion | flops 3225419776 | bytes 17301506 | tf_op jit(solution)/shard_map/dot_general | solution.py:41
  556.2 8.2 %collective-permute-done.48 = bf16[256,384]{1,0:T(8,128)(2,1)S(1)} collective-permute-done((bf16[256,384]{1,0:T(8,128)(2,1)S(1)}, bf16[256,384]{1,0:T(8,128)(2,1)S(1)}, u32[]{:S(2)}, u32[]{:S(2)}) %collective-permute-start.48) | collective-permute-done | bytes 196640 | tf_op jit(solution)/shard_map/ppermute | solution.py:72
  583.3 9.5 %all-to-all-done.5 = bf16[8,64,704]{2,1,0:T(8,128)(2,1)S(1)} async-done(((bf16[8,64,704]{2,1,0:T(8,128)(2,1)}), bf16[8,64,704]{2,1,0:T(8,128)(2,1)S(1)}, u32[]{:S(2)}, u32[]{:S(2)}) %all-to-all-start.5) | async-done | bytes 720928 | tf_op jit(solution)/shard_map/all_to_all | solution.py:117
  618.6 8.0 %all-to-all-done.6.refs_0_ = bf16[8,64,1152]{2,1,0:T(8,128)(2,1)} async-done(((bf16[8,64,1152]{2,1,0:T(8,128)(2,1)}), bf16[8,64,1152]{2,1,0:T(8,128)(2,1)}, u32[]{:S(2)}, u32[]{:S(2)}) %all-to-all-start.6) | async-done | bytes 1179680 | tf_op jit(solution)/shard_map/all_to_all | solution.py:117
  (480 shorter events, 327.1 us)
Async XLA Ops:
  7.2 53.8 %all-gather.5.cloned.1.call-start = ((), (), s32[]{:S(2)}) async-start(), calls=%async_computation.10 | async-start | bytes 2359296 | tf_op jit(solution)/shard_map/all_gather | solution.py:524
  12.1 47.1 %all-to-all-start = ((bf16[8,64,896]{2,1,0:T(8,128)(2,1)}), bf16[8,64,896]{2,1,0:T(8,128)(2,1)}, u32[]{:S(2)}, u32[]{:S(2)}) async-start(bf16[8,64,896]{2,1,0:T(8,128)(2,1)} %pad_maximum_fusion.1), calls=%async_computation | async-start | bytes 1835008 | tf_op jit(solution)/shard_map/all_to_all | solution.py:117
  18.5 103.2 %all-gather.7.cloned.1.call-start = ((), (), s32[]{:S(2)}) async-start(), calls=%async_computation.11 | async-start | bytes 5013504 | tf_op jit(solution)/shard_map/all_gather | solution.py:543
  124.8 50.9 %all-to-all-start.1 = ((bf16[8,64,1408]{2,1,0:T(8,128)(2,1)}), bf16[8,64,1408]{2,1,0:T(8,128)(2,1)S(1)}, u32[]{:S(2)}, u32[]{:S(2)}) async-start(bf16[8,64,1408]{2,1,0:T(8,128)(2,1)} %broadcast_add_fusion.1), calls=%async_computation.1 | async-start | bytes 2883584 | tf_op jit(solution)/shard_map/all_to_all | solution.py:117
  146.1 36.8 %collective-permute-start.5 = (bf16[2,128,2048]{2,1,0:T(8,128)(2,1)}, bf16[2,128,2048]{2,1,0:T(8,128)(2,1)}, u32[]{:S(2)}, u32[]{:S(2)}) collective-permute-start(bf16[2,128,2048]{2,1,0:T(8,128)(2,1)} %collective-permute-done.4.refs_3_), channel_id=1, source_target_pairs={{0,1},{1,0},{2,3},{3,2},{4,5},{5,4},{6,7},{7,6},{8,9},{9,8},{10,11... | collective-permute-start | bytes 3145736 | tf_op jit(solution)/shard_map/ppermute | solution.py:72
  146.2 44.7 %collective-permute-start.7 = (bf16[2,128,2048]{2,1,0:T(8,128)(2,1)}, bf16[2,128,2048]{2,1,0:T(8,128)(2,1)}, u32[]{:S(2)}, u32[]{:S(2)}) collective-permute-start(bf16[2,128,2048]{2,1,0:T(8,128)(2,1)} %collective-permute-done.6.refs_5_), channel_id=1, source_target_pairs={{0,1},{1,0},{2,3},{3,2},{4,5},{5,4},{6,7},{7,6},{8,9},{9,8},{10,11... | collective-permute-start | bytes 3145736 | tf_op jit(solution)/shard_map/ppermute | solution.py:72
  177.8 33.0 %all-to-all-start.2 = ((bf16[8,64,704]{2,1,0:T(8,128)(2,1)}), bf16[8,64,704]{2,1,0:T(8,128)(2,1)S(1)}, u32[]{:S(2)}, u32[]{:S(2)}) async-start(bf16[8,64,704]{2,1,0:T(8,128)(2,1)} %broadcast_add_fusion.3), calls=%async_computation.2 | async-start | bytes 1572864 | tf_op jit(solution)/shard_map/all_to_all | solution.py:117
  182.0 77.6 %all-gather.9.cloned.1.call-start = ((), (), s32[]{:S(2)}) async-start(), calls=%async_computation.12 | async-start | bytes 4718592 | tf_op jit(solution)/shard_map/all_gather | solution.py:572
  182.9 25.8 %collective-permute-start.13 = (bf16[2,128,1408]{2,1,0:T(8,128)(2,1)S(1)}, bf16[2,128,1408]{2,1,0:T(8,128)(2,1)S(1)}, u32[]{:S(2)}, u32[]{:S(2)}) collective-permute-start(bf16[2,128,1408]{2,1,0:T(8,128)(2,1)S(1)} %broadcast_add_fusion.5), channel_id=1, source_target_pairs={{0,16},{8,24},{16,0},{24,8},{1,17},{9,25},{17,1},{25,9},{2,18},{10... | collective-permute-start | bytes 2162696 | tf_op jit(solution)/shard_map/ppermute | solution.py:72
  212.9 109.2 %all-gather.11.cloned.1.call-start = ((), (), s32[]{:S(2)}) async-start(), calls=%async_computation.13 | async-start | bytes 4718592 | tf_op jit(solution)/shard_map/all_gather | solution.py:505
  262.3 127.6 %reduce-scatter.4.cloned.1.call-start = ((), (), s32[]{:S(2)}) async-start(), calls=%async_computation.14 | async-start | bytes 4718592 | tf_op jit(solution)/shard_map/reduce_scatter | solution.py:509
  263.4 27.8 %collective-permute-start.16 = (bf16[1,128,1408]{2,1,0:T(8,128)(2,1)S(1)}, bf16[1,128,1408]{2,1,0:T(8,128)(2,1)S(1)}, u32[]{:S(2)}, u32[]{:S(2)}) collective-permute-start(bf16[1,128,1408]{2,1,0:T(8,128)(2,1)S(1)} %slice.561), channel_id=1, source_target_pairs={{0,16},{8,24},{16,0},{24,8},{1,17},{9,25},{17,1},{25,9},{2,18},{10... | collective-permute-start | bytes 1081352 | tf_op jit(solution)/shard_map/ppermute | solution.py:72
  264.9 27.8 %collective-permute-start.17 = (bf16[1,128,1408]{2,1,0:T(8,128)(2,1)S(1)}, bf16[1,128,1408]{2,1,0:T(8,128)(2,1)S(1)}, u32[]{:S(2)}, u32[]{:S(2)}) collective-permute-start(bf16[1,128,1408]{2,1,0:T(8,128)(2,1)S(1)} %slice.562), channel_id=1, source_target_pairs={{0,8},{8,0},{16,24},{24,16},{1,9},{9,1},{17,25},{25,17},{2,10},{10... | collective-permute-start | bytes 1081352 | tf_op jit(solution)/shard_map/ppermute | solution.py:72
  267.5 25.3 %collective-permute-start.18 = (bf16[1,128,1408]{2,1,0:T(8,128)(2,1)S(1)}, bf16[1,128,1408]{2,1,0:T(8,128)(2,1)S(1)}, u32[]{:S(2)}, u32[]{:S(2)}) collective-permute-start(bf16[1,128,1408]{2,1,0:T(8,128)(2,1)S(1)} %slice.563), channel_id=1, source_target_pairs={{0,16},{8,24},{16,0},{24,8},{1,17},{9,25},{17,1},{25,9},{2,18},{10... | collective-permute-start | bytes 1081352 | tf_op jit(solution)/shard_map/ppermute | solution.py:72
  269.9 44.9 %collective-permute-start.22 = (bf16[1,256,704]{2,1,0:T(8,128)(2,1)S(1)}, bf16[1,256,704]{2,1,0:T(8,128)(2,1)S(1)}, u32[]{:S(2)}, u32[]{:S(2)}) collective-permute-start(bf16[1,256,704]{2,1,0:T(8,128)(2,1)S(1)} %slice.570), channel_id=1, source_target_pairs={{0,16},{8,24},{16,0},{24,8},{1,17},{9,25},{17,1},{25,9},{2,18},{10... | collective-permute-start | bytes 1081352 | tf_op jit(solution)/shard_map/ppermute | solution.py:72
  341.1 160.4 %reduce-scatter.6.cloned.1.call-start = ((), (), s32[]{:S(2)}) async-start(), calls=%async_computation.15 | async-start | bytes 4718592 | tf_op jit(solution)/shard_map/reduce_scatter | solution.py:509
  408.9 47.4 %all-to-all-start.3 = ((bf16[8,256,256]{2,1,0:T(8,128)(2,1)}), bf16[8,256,256]{2,1,0:T(8,128)(2,1)S(1)}, u32[]{:S(2)}, u32[]{:S(2)}) async-start(bf16[8,256,256]{2,1,0:T(8,128)(2,1)} %bitcast.370), calls=%async_computation.5 | async-start | bytes 2097152 | tf_op jit(solution)/shard_map/all_to_all | solution.py:117
  460.2 39.5 %all-to-all-start.4 = ((bf16[8,64,1408]{2,1,0:T(8,128)(2,1)}), bf16[8,64,1408]{2,1,0:T(8,128)(2,1)}, u32[]{:S(2)}, u32[]{:S(2)}) async-start(bf16[8,64,1408]{2,1,0:T(8,128)(2,1)} %maximum_add_fusion), calls=%async_computation.6 | async-start | bytes 2883584 | tf_op jit(solution)/shard_map/all_to_all | solution.py:117
  464.5 168.4 %reduce-scatter.8.cloned.1.call-start = ((), (), s32[]{:S(2)}) async-start(), calls=%async_computation.16 | async-start | bytes 4718592 | tf_op jit(solution)/shard_map/reduce_scatter | solution.py:509
  469.7 25.8 %collective-permute-start.36 = (bf16[256,704]{1,0:T(8,128)(2,1)S(1)}, bf16[256,704]{1,0:T(8,128)(2,1)S(1)}, u32[]{:S(2)}, u32[]{:S(2)}) collective-permute-start(bf16[256,704]{1,0:T(8,128)(2,1)S(1)} %get-tuple-element.59), channel_id=1, source_target_pairs={{0,8},{8,0},{16,24},{24,16},{1,9},{9,1},{17,25},{25,17},{2,10},{10... | collective-permute-start | bytes 1081352 | tf_op jit(solution)/shard_map/ppermute | solution.py:72
  470.2 25.3 %collective-permute-start.41 = (bf16[256,704]{1,0:T(8,128)(2,1)S(1)}, bf16[256,704]{1,0:T(8,128)(2,1)S(1)}, u32[]{:S(2)}, u32[]{:S(2)}) collective-permute-start(bf16[256,704]{1,0:T(8,128)(2,1)S(1)} %get-tuple-element.62), channel_id=1, source_target_pairs={{0,16},{8,24},{16,0},{24,8},{1,17},{9,25},{17,1},{25,9},{2,18},{10... | collective-permute-start | bytes 1081352 | tf_op jit(solution)/shard_map/ppermute | solution.py:72
  542.9 31.1 %collective-permute-start.42 = (bf16[256,768]{1,0:T(8,128)(2,1)}, bf16[256,768]{1,0:T(8,128)(2,1)}, u32[]{:S(2)}, u32[]{:S(2)}) collective-permute-start(bf16[256,768]{1,0:T(8,128)(2,1)} %get-tuple-element.51), channel_id=1, source_target_pairs={{0,8},{8,0},{16,24},{24,16},{1,9},{9,1},{17,25},{25,17},{2,10},{10... | collective-permute-start | bytes 1179656 | tf_op jit(solution)/shard_map/ppermute | solution.py:72
  544.5 30.6 %collective-permute-start.47 = (bf16[256,768]{1,0:T(8,128)(2,1)}, bf16[256,768]{1,0:T(8,128)(2,1)}, u32[]{:S(2)}, u32[]{:S(2)}) collective-permute-start(bf16[256,768]{1,0:T(8,128)(2,1)} %get-tuple-element.54), channel_id=1, source_target_pairs={{0,16},{8,24},{16,0},{24,8},{1,17},{9,25},{17,1},{25,9},{2,18},{10... | collective-permute-start | bytes 1179656 | tf_op jit(solution)/shard_map/ppermute | solution.py:72
  592.8 33.9 %all-to-all-start.6 = ((bf16[8,64,1152]{2,1,0:T(8,128)(2,1)}), bf16[8,64,1152]{2,1,0:T(8,128)(2,1)}, u32[]{:S(2)}, u32[]{:S(2)}) async-start(bf16[8,64,1152]{2,1,0:T(8,128)(2,1)} %pad_maximum_fusion), calls=%async_computation.9 | async-start | bytes 2359296 | tf_op jit(solution)/shard_map/all_to_all | solution.py:117
  (118 other events, 1504.8 us)
Sparse Core Ops, SparseCore 0:
  9.7 50.4 all-gather.4
  64.0 48.4 all-gather.6
  213.0 46.4 all-gather.8
  262.5 45.9 all-gather.10
  341.2 48.6 reduce-scatter.3
  397.0 64.8 reduce-scatter.5
  513.9 50.3 reduce-scatter.7
